TPU v7x, 32 devices: a whole 2x2x4 slice. The times are simulated.
32 devices in a mesh: dp: 4 (over y, x), expert: 8 (over z, core).
Axes of the slice: x: 2, y: 2, z: 4, core: 2. Of those that a mesh axis runs over, the one named last changes fastest.
Arguments:
- hidden_in: bfloat16 [32, 2, 2880], P(('expert', 'dp')), may hold values from -6 to 6
- queries: bfloat16 [32, 2, 4096], P(('expert', 'dp')), may hold values from -2 to 2
- new_keys: bfloat16 [32, 2, 512], P(('expert', 'dp')), may hold values from -2 to 2
- new_values: bfloat16 [32, 2, 512], P(('expert', 'dp')), may hold values from -6 to 6
- key_cache: bfloat16 [32, 512, 512], P(('expert', 'dp')), may hold values from -2 to 2
- value_cache: bfloat16 [32, 512, 512], P(('expert', 'dp')), may hold values from -6 to 6
- prompt_lengths: int32 [32], P(('expert', 'dp')), may hold values from 64 to 512, as said below
- out_weight: bfloat16 [4096, 2880], P('expert'), may hold values from -0.375 to 0.375
- norm_gain: float32 [2880], replicated, may hold values from 0.1 to 1.9
- expert_ids: int32 [32, 2, 4], P('expert'), may hold values from 0 to 15, all different within a row; in each aligned block of 8 rows (0 to 7, 8 to 15, ..., all dimensions but the last counted through in order) at most 6 rows name the same one
- top_logits: bfloat16 [32, 2, 4], P('expert'), may hold values from -4 to 4
- gate_weight: bfloat16 [16, 2880, 2880], P('expert', None, 'dp'), may hold values from -0.109375 to 0.109375
- up_weight: bfloat16 [16, 2880, 2880], P('expert', None, 'dp'), may hold values from -0.109375 to 0.109375
- down_weight: bfloat16 [16, 2880, 2880], P('expert', 'dp'), may hold values from -0.109375 to 0.109375
Outputs:
- layer_out: bfloat16 [32, 2, 2880], P(('expert', 'dp'))
Inputs may be any that keep to these rules, and one draw needn't show every extreme that they name: `prompt_lengths`: some row has exactly 512 live slots. `expert_ids`: A row names 4 different experts at each position. Over the 4 rows held by one index of the expert axis and both positions, no expert is named more than 6 times, and in some such group one expert is named exactly 6 times.
All inputs are finite; a program needn't handle non-finite values.
Results may differ from a plain program's by a relative error of at most 0.02.
Values may be sent and summed in bfloat16 or wider, within the bound.
A program may use at most 128 MiB of HBM per device.

v0:
```python
import jax
import jax.numpy as jnp
from jax import lax
from jax.sharding import PartitionSpec as P

HQ = 64
KVH = 8
HD = 64


def attend_single(query_rows, fresh_keys, fresh_values, cache_keys, cache_values, length):
    step_count = query_rows.shape[0]
    cache_len = cache_keys.shape[0]
    keys_all = jnp.concatenate([cache_keys, fresh_keys], axis=0).reshape(
        cache_len + step_count, KVH, HD
    )
    values_all = jnp.concatenate([cache_values, fresh_values], axis=0).reshape(
        cache_len + step_count, KVH, HD
    )
    query_heads = query_rows.reshape(step_count, KVH, HQ // KVH, HD)
    scores = (
        jnp.einsum("sgqe,kge->sgqk", query_heads, keys_all, preferred_element_type=jnp.float32)
        * 0.125
    )
    position = jnp.arange(cache_len + step_count, dtype=jnp.int32)
    step_ids = jnp.arange(step_count, dtype=jnp.int32)
    visible = (position[None, :] < length) | (position[None, :] >= cache_len) & (
        position[None, :] - cache_len <= step_ids[:, None]
    )
    exp_scores = jnp.where(visible[:, None, None, :], jnp.exp(scores), jnp.zeros_like(scores))
    attn_probs = (exp_scores / jnp.sum(exp_scores, axis=-1, keepdims=True)).astype(jnp.bfloat16)
    attended = jnp.einsum(
        "sgqk,kge->sgqe", attn_probs, values_all, preferred_element_type=jnp.float32
    )
    return attended.astype(jnp.bfloat16).reshape(step_count, HQ * HD)


def rms_normed(residual, norm_gain):
    inverse_rms = lax.rsqrt(jnp.mean(residual * residual, axis=-1, keepdims=True) + 1e-05)
    return (residual * inverse_rms * norm_gain).astype(jnp.bfloat16)


def swiglu_act(gate_vals, up_vals):
    return (gate_vals * jax.nn.sigmoid(1.702 * gate_vals) * (up_vals + 1.0)).astype(jnp.bfloat16)


def expert_partials(slot_block, gate_weight, up_weight, down_weight):
    results = []
    for local_expert in range(slot_block.shape[1]):
        row_block = slot_block[:, local_expert].reshape(-1, slot_block.shape[3])
        gate_vals = jnp.dot(
            row_block, gate_weight[local_expert], preferred_element_type=jnp.float32
        )
        up_vals = jnp.dot(row_block, up_weight[local_expert], preferred_element_type=jnp.float32)
        activated = swiglu_act(gate_vals, up_vals)
        partial_out = jnp.dot(
            activated, down_weight[local_expert], preferred_element_type=jnp.float32
        )
        results.append(
            partial_out.reshape(slot_block.shape[0], slot_block.shape[2], slot_block.shape[3])
        )
    return jnp.stack(results, axis=1)


def routing_tables(chosen_ids, chosen_logits, experts_all, capacity):
    flat_ids = chosen_ids.reshape(-1, chosen_ids.shape[-1])
    exp_logits = jnp.exp(chosen_logits.reshape(flat_ids.shape).astype(jnp.float32))
    mix_weights = exp_logits / jnp.sum(exp_logits, axis=-1, keepdims=True)
    labels = jnp.arange(experts_all, dtype=jnp.int32)
    match_int = (flat_ids[:, :, None] == labels[None, None, :]).astype(jnp.int32)
    hits_int = jnp.sum(match_int, axis=1)
    slot_int = jnp.cumsum(hits_int, axis=0) - hits_int
    places = jnp.arange(capacity, dtype=jnp.int32)
    select = (
        hits_int.T[:, None, :] * (slot_int.T[:, None, :] == places[None, :, None]).astype(jnp.int32)
    ).astype(jnp.float32)
    token_slots = jnp.take_along_axis(slot_int, flat_ids, axis=1)
    source_rows = flat_ids * capacity + token_slots
    return (select, source_rows, mix_weights)


def gathered_combine(returned_flat, source_rows, mix_weights):
    picked = jnp.take(returned_flat, source_rows.reshape(-1), axis=0)
    picked = picked.reshape(source_rows.shape[0], source_rows.shape[1], returned_flat.shape[1])
    return jnp.sum(picked * mix_weights[:, :, None], axis=1)


def on_device(
    hidden_in,
    queries,
    new_keys,
    new_values,
    key_cache,
    value_cache,
    prompt_lengths,
    out_weight,
    norm_gain,
    expert_ids,
    top_logits,
    gate_weight,
    up_weight,
    down_weight,
):
    row_dev = hidden_in.shape[0]
    step_count = hidden_in.shape[1]
    model_width = hidden_in.shape[2]
    per_index = gate_weight.shape[0]
    expert_group = lax.axis_size("expert")
    experts_all = per_index * expert_group
    attended = jax.vmap(attend_single)(
        queries, new_keys, new_values, key_cache, value_cache, prompt_lengths
    )
    by_heads = lax.all_to_all(attended, "expert", split_axis=2, concat_axis=0, tiled=True)
    projected = lax.psum_scatter(
        jnp.einsum("rsf,fd->rsd", by_heads, out_weight, preferred_element_type=jnp.float32).astype(
            jnp.bfloat16
        ),
        "expert",
        scatter_dimension=0,
        tiled=True,
    ).astype(jnp.float32)
    residual = hidden_in.astype(jnp.float32) + projected
    normed = rms_normed(residual, norm_gain)
    capacity = row_dev * step_count
    start_row = lax.axis_index("dp") * row_dev
    mine_ids = lax.dynamic_slice_in_dim(expert_ids, start_row, row_dev, 0)
    mine_logits = lax.dynamic_slice_in_dim(top_logits, start_row, row_dev, 0)
    select, source_rows, mix_weights = routing_tables(mine_ids, mine_logits, experts_all, capacity)
    dispatch = jnp.einsum(
        "xct,td->xcd",
        select.astype(jnp.bfloat16),
        normed.reshape(-1, model_width),
        preferred_element_type=jnp.float32,
    )
    dispatch = dispatch.astype(jnp.bfloat16).reshape(expert_group, per_index, capacity, model_width)
    arrived = lax.all_to_all(dispatch, "expert", split_axis=0, concat_axis=0, tiled=True)
    partials = expert_partials(
        lax.all_gather(arrived, "dp", axis=0, tiled=True), gate_weight, up_weight, down_weight
    )
    summed = lax.psum_scatter(
        partials.astype(jnp.bfloat16), "dp", scatter_dimension=0, tiled=True
    ).astype(jnp.float32)
    returned = lax.all_to_all(
        summed.astype(jnp.bfloat16), "expert", split_axis=0, concat_axis=0, tiled=True
    ).astype(summed.dtype)
    moe_flat = gathered_combine(
        returned.reshape(experts_all * capacity, model_width), source_rows, mix_weights
    )
    moe_out = moe_flat.reshape(row_dev, step_count, model_width)
    return (residual + moe_out).astype(jnp.bfloat16)


def solution(mesh):
    placed = (
        P(("expert", "dp"), None, None),
        P(("expert", "dp"), None, None),
        P(("expert", "dp"), None, None),
        P(("expert", "dp"), None, None),
        P(("expert", "dp"), None, None),
        P(("expert", "dp"), None, None),
        P(("expert", "dp")),
        P("expert", None),
        P(),
        P("expert", None, None),
        P("expert", None, None),
        P("expert", None, "dp"),
        P("expert", None, "dp"),
        P("expert", "dp", None),
    )
    return jax.shard_map(
        on_device,
        mesh=mesh,
        in_specs=placed,
        out_specs=P(("expert", "dp"), None, None),
        check_vma=False,
    )
```

profile of v0, /device:TPU:0, one launch (start us, length us, event | category | flops | bytes accessed | tf_op | source)
XLA Modules:
  0.0 245.9 jit_solution(12194986989052161839)
XLA Ops:
  13.3 1.4 fusion.52
  14.8 3.8 %copy.58 = bf16[1,2,4096]{1,0,2:T(2,128)(2,1)} copy(bf16[1,2,4096]{2,1,0:T(2,128)(2,1)S(1)} %reshape.327) | data formatting | bytes 32768 | tf_op jit(solution)/shard_map/vmap()/reshape | solution.py:35
  19.2 24.4 %reduce.3 = bf16[4096,2]{1,0:T(8,128)(2,1)} reduce(bf16[4096,1,2]{2,1,0:T(2,128)(2,1)} %bitcast.124, bf16[]{:T(256)} %broadcast.310), dimensions={1}, to_apply=%bitcast.115.reduce_sub_computation | reduce | bytes 32770
  43.6 3.3 %reshape.365 = bf16[8,2,512]{2,1,0:T(2,128)(2,1)} reshape(bf16[4096,2]{1,0:T(8,128)(2,1)} %reduce.3) | data formatting | bytes 32768
  47.0 6.3 %all-to-all-start = ((bf16[8,2,512]{2,1,0:T(2,128)(2,1)}), bf16[8,2,512]{2,1,0:T(2,128)(2,1)S(1)}, u32[]{:S(2)}, u32[]{:S(2)}) async-start(bf16[8,2,512]{2,1,0:T(2,128)(2,1)} %reshape.365), calls=%async_computation | async-start | bytes 32768 | tf_op jit(solution)/shard_map/all_to_all | solution.py:113
  54.1 4.8 %all-to-all-done = bf16[8,2,512]{2,1,0:T(2,128)(2,1)S(1)} async-done(((bf16[8,2,512]{2,1,0:T(2,128)(2,1)}), bf16[8,2,512]{2,1,0:T(2,128)(2,1)S(1)}, u32[]{:S(2)}, u32[]{:S(2)}) %all-to-all-start) | async-done | bytes 16416 | tf_op jit(solution)/shard_map/all_to_all | solution.py:113
  58.9 4.3 %reshape.366 = bf16[4096,1,2]{2,1,0:T(2,128)(2,1)} reshape(bf16[8,2,512]{2,1,0:T(2,128)(2,1)S(1)} %all-to-all-done) | data formatting | bytes 32768
  63.3 4.5 %copy.59 = bf16[1,2,4096]{2,1,0:T(2,128)(2,1)S(1)} copy(bf16[1,2,4096]{1,0,2:T(2,128)(2,1)} %bitcast.125) | data formatting | bytes 32768 | tf_op jit(solution)/shard_map/all_to_all | solution.py:113
  70.1 49.4 %all-reduce.5.cloned.1.call-done = bf16[8,2,2880]{2,1,0:T(2,128)(2,1)} async-done(((bf16[8,2,2880]{2,1,0:T(2,128)(2,1)}), bf16[8,2,2880]{2,1,0:T(2,128)(2,1)}) %all-reduce.5.cloned.1.call-update) | async-done | bytes 92176
  119.5 1.5 multiply_reduce_fusion.1
  121.0 1.6 convolution_convert_fusion
  122.8 13.1 %all_to_all.28 = bf16[8,2,2,2880]{3,2,1,0:T(2,128)(2,1)S(1)} all-to-all(bf16[8,2,2,2880]{3,2,1,0:T(2,128)(2,1)S(1)} %bitcast.127), channel_id=1, replica_groups=mesh['dp'=4,'expert'=8] {'expert'}, dimensions={0} | all-to-all | bytes 368640 | tf_op jit(solution)/shard_map/all_to_all | solution.py:136
  135.9 11.3 %all_gather.3 = bf16[32,2,2,2880]{3,2,1,0:T(2,128)(2,1)S(1)} all-gather(bf16[8,2,2,2880]{3,2,1,0:T(2,128)(2,1)S(1)} %all_to_all.28), channel_id=1, replica_groups=mesh['dp'=4,'expert'=8] {'dp'}, dimensions={0}, use_global_device_ids=true | all-gather | bytes 921600 | tf_op jit(solution)/shard_map/all_gather | solution.py:138
  148.4 2.0 reshape_squeeze.7
  150.4 3.7 %fusion.4 = f32[64,720]{1,0:T(8,128)S(1)} fusion(bf16[64,2880]{1,0:T(8,128)(2,1)} %reshape_squeeze.7, bf16[2,2880,720]{1,2,0:T(8,128)(2,1)} %param.25), kind=kOutput, calls=%fused_computation.6 | convolution fusion | flops 265420800 | bytes 4800512 | tf_op jit(solution)/shard_map/dot_general | solution.py:51
  154.2 4.2 %fusion.46 = bf16[64,720]{1,0:T(8,128)(2,1)} fusion(bf16[64,2880]{1,0:T(8,128)(2,1)S(1)} %copy-done.1, bf16[2,2880,720]{1,2,0:T(8,128)(2,1)} %param.26, f32[64,720]{1,0:T(8,128)S(1)} %fusion.4), kind=kOutput, calls=%fused_computation.35 | convolution fusion | flops 265789440 | bytes 4884480 | tf_op jit(solution)/shard_map/dot_general | solution.py:54
  160.3 3.7 %fusion.10 = f32[64,720]{1,0:T(8,128)S(1)} fusion(bf16[64,2880]{1,0:T(8,128)(2,1)} %reshape_squeeze.6, bf16[2,2880,720]{1,2,0:T(8,128)(2,1)} %param.25), kind=kOutput, calls=%fused_computation.12 | convolution fusion | flops 265420800 | bytes 4800512 | tf_op jit(solution)/shard_map/dot_general | solution.py:51
  164.1 3.6 %fusion.49 = bf16[64,720]{1,0:T(8,128)(2,1)S(1)} fusion(bf16[64,2880]{1,0:T(8,128)(2,1)S(1)} %copy-done.2, bf16[2,2880,720]{1,2,0:T(8,128)(2,1)} %param.26, f32[64,720]{1,0:T(8,128)S(1)} %fusion.10), kind=kOutput, calls=%fused_computation.36 | convolution fusion | flops 265789440 | bytes 4884480 | tf_op jit(solution)/shard_map/dot_general | solution.py:54
  167.7 3.0 %fusion.24 = bf16[32,1,2,2880]{3,0,2,1:T(8,128)(2,1)S(1)} fusion(bf16[2,720,2880]{2,1,0:T(8,128)(2,1)} %param.27, bf16[32,2,720]{2,1,0:T(2,128)(2,1)S(1)} %reshape.333), kind=kOutput, calls=%fused_computation.22 | convolution fusion | flops 265605120 | bytes 4700160 | tf_op jit(solution)/shard_map/dot_general | solution.py:56
  170.8 3.0 %fusion.27 = bf16[32,1,2,2880]{3,0,2,1:T(8,128)(2,1)S(1)} fusion(bf16[2,720,2880]{2,1,0:T(8,128)(2,1)} %param.27, bf16[32,2,720]{2,1,0:T(2,128)(2,1)S(1)} %reshape.332), kind=kOutput, calls=%fused_computation.23 | convolution fusion | flops 265605120 | bytes 4700160 | tf_op jit(solution)/shard_map/dot_general | solution.py:56
  177.1 44.5 %all-reduce.7.cloned.1.call-done = bf16[32,2,2,2880]{3,0,2,1:T(8,128)(2,1)} async-done(((bf16[32,2,2,2880]{3,0,2,1:T(8,128)(2,1)}), bf16[32,2,2,2880]{3,0,2,1:T(8,128)(2,1)}) %all-reduce.7.cloned.1.call-update) | async-done | bytes 737296
  223.4 4.6 %all-to-all-start.2 = ((bf16[8,2,2,2880]{3,2,1,0:T(2,128)(2,1)}), bf16[8,2,2,2880]{3,2,1,0:T(2,128)(2,1)S(1)}, u32[]{:S(2)}, u32[]{:S(2)}) async-start(bf16[8,2,2,2880]{3,2,1,0:T(2,128)(2,1)} %copy.64), calls=%async_computation.2 | async-start | bytes 376832 | tf_op jit(solution)/shard_map/all_to_all | solution.py:143
  228.1 8.1 %all-to-all-done.2 = bf16[8,2,2,2880]{3,2,1,0:T(2,128)(2,1)S(1)} async-done(((bf16[8,2,2,2880]{3,2,1,0:T(2,128)(2,1)}), bf16[8,2,2,2880]{3,2,1,0:T(2,128)(2,1)S(1)}, u32[]{:S(2)}, u32[]{:S(2)}) %all-to-all-start.2) | async-done | bytes 184352 | tf_op jit(solution)/shard_map/all_to_all | solution.py:143
  237.1 2.0 fusion.57
  (65 shorter events, 18.5 us)
Async XLA Ops:
  6.5 61.3 %copy-start = (bf16[512,2880]{0,1:T(8,128)(2,1)S(1)}, bf16[512,2880]{0,1:T(8,128)(2,1)}, u32[]{:S(2)}) copy-start(bf16[512,2880]{0,1:T(8,128)(2,1)} %param.21) | copy-start | bytes 8847364
  6.5 4.5 %copy-start.4 = (bf16[1,2,4096]{2,1,0:T(2,128)(2,1)S(1)}, bf16[1,2,4096]{2,1,0:T(2,128)(2,1)}, u32[]{:S(2)}) copy-start(bf16[1,2,4096]{2,1,0:T(2,128)(2,1)} %param.15) | copy-start | bytes 49156
  43.6 25.9 %copy-start.8 = (u32[32]{0:T(128)S(1)}, u32[32]{0:T(128)}, u32[]{:S(2)}) copy-start(u32[32]{0:T(128)} %constant.90) | copy-start | bytes 388
  43.6 75.9 %copy-start.3 = (bf16[1,2,2880]{2,1,0:T(2,128)(2,1)S(1)}, bf16[1,2,2880]{2,1,0:T(2,128)(2,1)}, u32[]{:S(2)}) copy-start(bf16[1,2,2880]{2,1,0:T(2,128)(2,1)} %param.14) | copy-start | bytes 34564
  43.6 77.4 %copy-start.5 = (f32[2880]{0:T(1024)S(1)}, f32[2880]{0:T(1024)}, u32[]{:S(2)}) copy-start(f32[2880]{0:T(1024)} %param.22) | copy-start | bytes 34564
  47.0 12.0 %all-to-all-start = ((bf16[8,2,512]{2,1,0:T(2,128)(2,1)}), bf16[8,2,512]{2,1,0:T(2,128)(2,1)S(1)}, u32[]{:S(2)}, u32[]{:S(2)}) async-start(bf16[8,2,512]{2,1,0:T(2,128)(2,1)} %reshape.365), calls=%async_computation | async-start | bytes 32768 | tf_op jit(solution)/shard_map/all_to_all | solution.py:113
  53.3 66.2 %all-reduce.5.cloned.1.call-start = ((), (), s32[]{:S(2)}) async-start(), calls=%async_computation.3 | async-start | bytes 188416
  69.4 152.3 %all-reduce.7.cloned.1.call-start = ((), (), s32[]{:S(2)}) async-start(), calls=%async_computation.4 | async-start | bytes 1507328
  150.4 3.7 %copy-start.1 = (bf16[64,2880]{1,0:T(8,128)(2,1)S(1)}, bf16[64,2880]{1,0:T(8,128)(2,1)}, u32[]{:S(2)}) copy-start(bf16[64,2880]{1,0:T(8,128)(2,1)} %reshape_squeeze.7) | copy-start | bytes 1105924
  160.3 3.7 %copy-start.2 = (bf16[64,2880]{1,0:T(8,128)(2,1)S(1)}, bf16[64,2880]{1,0:T(8,128)(2,1)}, u32[]{:S(2)}) copy-start(bf16[64,2880]{1,0:T(8,128)(2,1)} %reshape_squeeze.6) | copy-start | bytes 1105924
  170.7 4.1 %copy-start.7 = (u32[32]{0:T(128)S(1)}, u32[32]{0:T(128)}, u32[]{:S(2)}) copy-start(u32[32]{0:T(128)} %constant.94) | copy-start | bytes 388
  170.7 6.2 %copy-start.6 = (bf16[4,2,4]{2,1,0:T(2,128)(2,1)S(1)}, bf16[4,2,4]{2,1,0:T(2,128)(2,1)}, u32[]{:S(2)}) copy-start(bf16[4,2,4]{2,1,0:T(2,128)(2,1)} %param.24) | copy-start | bytes 196
  223.4 12.8 %all-to-all-start.2 = ((bf16[8,2,2,2880]{3,2,1,0:T(2,128)(2,1)}), bf16[8,2,2,2880]{3,2,1,0:T(2,128)(2,1)S(1)}, u32[]{:S(2)}, u32[]{:S(2)}) async-start(bf16[8,2,2,2880]{3,2,1,0:T(2,128)(2,1)} %copy.64), calls=%async_computation.2 | async-start | bytes 376832 | tf_op jit(solution)/shard_map/all_to_all | solution.py:143
Sparse Core Ops, SparseCore 0:
  69.5 49.9 all-reduce.4
  174.9 46.7 all-reduce.6
where the time goes:
time: 247 us; the launch traced here: 246 us
  waiting for transfers between devices  107 us (43%)
  other arithmetic  32.4 us (13%)
  local copies, waits for them, and re-layouts  29.7 us (12%)
  matrix products  26.6 us (11%)
  blocking collectives  24.4 us (10%)
  between operations  14.9 us (6%)
  starting transfers between devices  11 us (4%)
    unnamed x4, waiting for transfers between devices  94 us
    unnamed x1, other arithmetic  24.4 us
    all_to_all x1, blocking collectives, on_device(): lax.all_to_all(dispatch, 'expert', split_axis=0, concat_axis=0, tiled=True)  13.1 us
    all_gather x1, blocking collectives, on_device(): lax.all_gather(arrived, 'dp', axis=0, tiled=True)  11.3 us
    unnamed x24, local copies, waits for them, and re-layouts  10.4 us
    all_to_all x1, waiting for transfers between devices, on_device(): lax.all_to_all(summed.astype(jnp.bfloat16), 'expert', split_axis=0, conca...  8.14 us
    dot_general x2, matrix products, expert_partials(): jnp.dot(row_block, up_weight[local_expert], preferred_element_type=jnp.fl...  7.8 us
    dot_general x2, matrix products, expert_partials(): jnp.dot(row_block, gate_weight[local_expert], preferred_element_type=jnp....  7.48 us
  transfers between devices with their start and end apart: 4, of which 4 were waited for; matrix products, arithmetic and copies ran while one was open for 1% of the time, Pallas kernels for 0%

commit v1 on v0

v1 whole, which is shorter than its diff:
```python
import functools

import jax
import jax.numpy as jnp
from jax import lax
from jax.experimental import pallas as pl
from jax.experimental.pallas import tpu as pltpu
from jax.sharding import PartitionSpec as P

KVH = 8
HD = 64
MESH = pl.DeviceIdType.MESH
F32 = jnp.float32
BF16 = jnp.bfloat16


def iota(shape, dim):
    return lax.broadcasted_iota(jnp.int32, shape, dim)


def dot_last(a, b):
    return lax.dot_general(a, b, (((1,), (1,)), ((), ())), preferred_element_type=F32)


def dot(a, b):
    return jnp.dot(a, b, preferred_element_type=F32)


def layer_kernel(
    n_dp, n_ex, per_index, cuts,
    plen_ref, hid_ref, q_ref, nk_ref, nv_ref, gain_ref, ids_ref, lg_ref,
    kc_hbm, vc_hbm, wo_hbm, wg_hbm, wu_hbm, wd_hbm,
    out_ref,
    kbuf, vbuf, wo, wg, wu, wd,
    qr, att, send_att, recv_att, xa, part, send_proj, recv_proj, resid,
    xbuf, xs, send_dp, recv_dp, send_out, recv_out,
    load_sem, ssem, rsem, fssem, frsem, hssem, hrsem,
):
    me_dp = lax.axis_index("dp")
    me_ex = lax.axis_index("expert")
    steps, width = hid_ref.shape[1], hid_ref.shape[2]
    feats = wo.shape[1]
    pad_at = xbuf.shape[3] - 128

    loads = [(kc_hbm.at[0], kbuf), (vc_hbm.at[0], vbuf), (wo_hbm, wo)]
    for l in range(per_index):
        loads += [(wg_hbm.at[l], wg.at[l]), (wu_hbm.at[l], wu.at[l]), (wd_hbm.at[l], wd.at[l])]
    loads = [pltpu.make_async_copy(s, d, load_sem.at[i]) for i, (s, d) in enumerate(loads)]
    for c in loads[:3]:
        c.start()

    barrier = pltpu.get_barrier_semaphore()
    for d in range(1, n_ex):
        pl.semaphore_signal(barrier, inc=1, device_id=(me_dp, lax.rem(me_ex + d, n_ex)), device_id_type=MESH)
    for d in range(1, n_dp):
        pl.semaphore_signal(barrier, inc=1, device_id=(lax.rem(me_dp + d, n_dp), me_ex), device_id_type=MESH)

    rows, lanes = 2 * KVH * 8, KVH * HD
    for g in range(KVH):
        qr[2 * g:2 * g + 2, :] = q_ref[0, :, g * lanes:(g + 1) * lanes].astype(F32)
    r_of, l_of = iota((rows, lanes), 0), iota((rows, lanes), 1)
    own_head = (l_of // HD) == (r_of % 8)
    own_group = (l_of // HD) == ((r_of % 64) // 8)
    repeat = ((iota((lanes, lanes), 0) % HD) == (iota((lanes, lanes), 1) % HD)).astype(F32).astype(BF16)
    er, ei = iota((rows, 16), 0), iota((rows, 16), 1)
    spread = (((er % 64) // 8 == ei // 2) & (er // 64 == ei % 2)).astype(F32).astype(BF16)
    fi, fr = iota((16, rows), 0), iota((16, rows), 1)
    collect = (((fr % 64) // 8 == fi // 2) & (fr // 64 == fi % 2)).astype(F32).astype(BF16)
    a = dot(spread, qr[...].astype(BF16))
    a = jnp.where(own_head, a, 0.0).astype(BF16)
    a = jnp.where(own_group, dot(a, repeat), 0.0).astype(BF16)
    nrow = iota((128, lanes), 0)

    def padded(ref):
        v = ref[0].astype(F32)
        return jnp.where(nrow == 0, v[0:1], jnp.where(nrow == 1, v[1:2], 0.0)).astype(BF16)

    sn = dot_last(a, padded(nk_ref)) * 0.125
    en = jnp.where(iota(sn.shape, 1) <= iota(sn.shape, 0) // 64, jnp.exp(sn), 0.0)
    loads[0].wait()
    sc = dot_last(a, kbuf[...]) * 0.125
    ec = jnp.where(iota(sc.shape, 1) < plen_ref[0], jnp.exp(sc), 0.0)
    den = jnp.sum(ec, axis=1, keepdims=True) + jnp.sum(en, axis=1, keepdims=True)
    loads[1].wait()
    for c in loads[3:]:
        c.start()
    o = dot((ec / den).astype(BF16), vbuf[...]) + dot((en / den).astype(BF16), padded(nv_ref))
    o = jnp.where(own_group, o, 0.0).astype(BF16)
    o = jnp.where(own_head, dot(o, repeat), 0.0).astype(BF16)
    att[...] = dot(collect, o)
    for e in range(n_ex):
        g, at = e * feats // lanes, e * feats % lanes
        send_att[e] = att[2 * g:2 * g + 2, at:at + feats].astype(BF16)
    recv_att[me_ex] = send_att[me_ex]

    pl.semaphore_wait(barrier, n_ex - 1 + n_dp - 1)

    def exchange(phase, send, recv):
        for d in range(1, n_ex):
            to = lax.rem(me_ex + d, n_ex)
            pltpu.make_async_remote_copy(
                send.at[to], recv.at[me_ex], ssem.at[phase, d], rsem.at[phase, me_ex],
                device_id=(me_dp, to), device_id_type=MESH,
            ).start()

    def exchanged(phase, send, recv):
        for d in range(1, n_ex):
            src = lax.rem(me_ex + d, n_ex)
            c = pltpu.make_async_remote_copy(
                send.at[src], recv.at[src], ssem.at[phase, d], rsem.at[phase, src],
                device_id=(me_dp, src), device_id_type=MESH,
            )
            c.wait_recv()
            c.wait_send()

    exchange(0, send_att, recv_att)

    logit = jnp.exp(lg_ref[me_dp].astype(F32))
    mix = logit / jnp.sum(logit, axis=1, keepdims=True)
    ids = ids_ref[me_dp]
    lane = iota((steps, 128), 1)
    dense = jnp.zeros((steps, 128), F32)
    for k in range(ids.shape[1]):
        dense = dense + jnp.where((lane % 64) == ids[:, k:k + 1], mix[:, k:k + 1], 0.0)
    high = dense.astype(BF16).astype(F32)
    dense = jnp.where(lane < 64, high, dense - high).astype(BF16)

    loads[2].wait()
    exchanged(0, send_att, recv_att)
    for e in range(n_ex):
        xa[2 * e:2 * e + 2, :] = recv_att[e].astype(F32)
    part[...] = dot_last(xa[...].astype(BF16), wo[...])
    for e in range(n_ex):
        send_proj[e] = part[2 * e:2 * e + 2, :].astype(BF16)
    recv_proj[me_ex] = send_proj[me_ex]
    exchange(1, send_proj, recv_proj)
    xbuf[me_dp, me_ex, :, width:pad_at] = jnp.zeros((steps, pad_at - width), BF16)
    xbuf[me_dp, me_ex, :, pad_at:] = dense
    exchanged(1, send_proj, recv_proj)
    res = hid_ref[0].astype(F32) + jnp.sum(recv_proj[...].astype(F32), axis=0)
    resid[...] = res
    inv = lax.rsqrt(jnp.sum(res * res, axis=1, keepdims=True) / width + 1e-05)
    xbuf[me_dp, me_ex, :, 0:width] = (res * inv * gain_ref[...].reshape(1, width)).astype(BF16)

    def to_expert(slab, d, peer):
        return pltpu.make_async_remote_copy(
            xbuf.at[me_dp, slab], xbuf.at[me_dp, slab], ssem.at[2, d], rsem.at[2, slab],
            device_id=(me_dp, peer), device_id_type=MESH,
        )

    def to_dp(row, slab, d, peer):
        return pltpu.make_async_remote_copy(
            xbuf.at[row, slab], xbuf.at[row, slab], fssem.at[slab, d], frsem.at[slab, row],
            device_id=(peer, me_ex), device_id_type=MESH,
        )

    def pass_on(slab):
        for d in range(1, n_dp):
            to_dp(me_dp, slab, d, lax.rem(me_dp + d, n_dp)).start()

    for d in range(1, n_ex):
        to_expert(me_ex, d, lax.rem(me_ex + d, n_ex)).start()
    pass_on(me_ex)
    for d in range(1, n_ex):
        src = lax.rem(me_ex + d, n_ex)
        to_expert(src, d, src).wait_recv()
        pass_on(src)
    for e in range(n_ex):
        xs[me_dp, 2 * e:2 * e + 2, :] = xbuf[me_dp, e].astype(F32)
    for d in range(1, n_dp):
        row = lax.rem(me_dp + d, n_dp)
        for e in range(n_ex):
            to_dp(row, e, d, row).wait_recv()
            xs[row, 2 * e:2 * e + 2, :] = xbuf[row, e].astype(F32)
    for d in range(1, n_ex):
        to_expert(me_ex, d, me_ex).wait_send()
    for d in range(1, n_dp):
        for e in range(n_ex):
            to_dp(me_dp, e, d, me_dp).wait_send()

    for c in loads[3:]:
        c.wait()
    span = max(1, min(n_dp, 64 // (2 * n_ex)))
    tokens = span * 2 * n_ex

    def block(at):
        x = xs[pl.ds(at, span), :, 0:width].reshape(tokens, width).astype(BF16)
        shares = xs[pl.ds(at, span), :, pad_at:].reshape(tokens, 128)
        lane_of = iota((tokens, 128), 1) % 64
        acts, parts = [], []
        for l in range(per_index):
            gate = dot_last(x, wg[l])
            up = dot_last(x, wu[l])
            acts.append((gate * jax.nn.sigmoid(1.702 * gate) * (up + 1.0)).astype(BF16))
            mine = lane_of == me_ex * per_index + l
            parts.append(jnp.sum(jnp.where(mine, shares, 0.0), axis=1, keepdims=True))
        for c, (lo, hi) in enumerate(cuts):
            total = dot(acts[0], wd[0, :, lo:hi]) * parts[0]
            for l in range(1, per_index):
                total = total + dot(acts[l], wd[l, :, lo:hi]) * parts[l]
            send_dp[c][pl.ds(at, span)] = total.reshape(span, 2 * n_ex, hi - lo).astype(BF16)
            if n_dp == span:
                scatter(c)

    def across(c, d, slot):
        to = lax.rem(me_dp + d, n_dp)
        return pltpu.make_async_remote_copy(
            send_dp[c].at[to], recv_dp[c].at[slot], hssem.at[c, d], hrsem.at[c, slot],
            device_id=(to, me_ex), device_id_type=MESH,
        )

    def scatter(c):
        for d in range(1, n_dp):
            across(c, d, me_dp).start()
        recv_dp[c][me_dp] = send_dp[c][me_dp]

    if n_dp == span:
        block(0)
    else:
        pl.loop(0, n_dp // span)(lambda i: block(i * span))
        for c in range(len(cuts)):
            scatter(c)

    for c, (lo, hi) in enumerate(cuts):
        for d in range(1, n_dp):
            across(c, d, lax.rem(me_dp + d, n_dp)).wait_recv()
        part[:, lo:hi] = jnp.sum(recv_dp[c][...].astype(F32), axis=0)
        for e in range(n_ex):
            send_out[c][e] = part[2 * e:2 * e + 2, lo:hi].astype(BF16)
        exchange(3 + c, send_out[c], recv_out[c])
        recv_out[c][me_ex] = send_out[c][me_ex]
    for c in range(len(cuts)):
        for d in range(1, n_dp):
            across(c, d, me_dp).wait_send()
    for c, (lo, hi) in enumerate(cuts):
        exchanged(3 + c, send_out[c], recv_out[c])
        moe = jnp.sum(recv_out[c][...].astype(F32), axis=0)
        out_ref[0, :, lo:hi] = (resid[:, lo:hi] + moe).astype(BF16)


def on_device(
    hidden_in, queries, new_keys, new_values, key_cache, value_cache, prompt_lengths,
    out_weight, norm_gain, expert_ids, top_logits, gate_weight, up_weight, down_weight,
):
    n_dp, n_ex = lax.axis_size("dp"), lax.axis_size("expert")
    per_index = gate_weight.shape[0]
    width = hidden_in.shape[2]
    feats = out_weight.shape[0]
    half = -(-width // 256) * 128
    cuts = ((0, half), (half, width))
    gate_weight, up_weight = jnp.swapaxes(gate_weight, 1, 2), jnp.swapaxes(up_weight, 1, 2)
    out_weight = out_weight.T
    padded = -(-width // 128) * 128 + 128
    toks = 2 * n_ex
    vm, anym = pl.BlockSpec(memory_space=pltpu.VMEM), pl.BlockSpec(memory_space=pl.ANY)
    dma = pltpu.SemaphoreType.DMA
    return pl.pallas_call(
        functools.partial(layer_kernel, n_dp, n_ex, per_index, cuts),
        out_shape=jax.ShapeDtypeStruct(hidden_in.shape, BF16),
        in_specs=[pl.BlockSpec(memory_space=pltpu.SMEM)] + [vm] * 7 + [anym] * 6,
        out_specs=vm,
        scratch_shapes=[
            pltpu.VMEM(key_cache.shape[1:], BF16),
            pltpu.VMEM(value_cache.shape[1:], BF16),
            pltpu.VMEM(out_weight.shape, BF16),
            pltpu.VMEM(gate_weight.shape, BF16),
            pltpu.VMEM(up_weight.shape, BF16),
            pltpu.VMEM(down_weight.shape, BF16),
            pltpu.VMEM((16, KVH * HD), F32),
            pltpu.VMEM((16, KVH * HD), F32),
            pltpu.VMEM((n_ex, 2, feats), BF16),
            pltpu.VMEM((n_ex, 2, feats), BF16),
            pltpu.VMEM((toks, feats), F32),
            pltpu.VMEM((toks, width), F32),
            pltpu.VMEM((n_ex, 2, width), BF16),
            pltpu.VMEM((n_ex, 2, width), BF16),
            pltpu.VMEM((2, width), F32),
            pltpu.VMEM((n_dp, n_ex, 2, padded), BF16),
            pltpu.VMEM((n_dp, toks, padded), F32),
            [pltpu.VMEM((n_dp, toks, hi - lo), BF16) for lo, hi in cuts],
            [pltpu.VMEM((n_dp, toks, hi - lo), BF16) for lo, hi in cuts],
            [pltpu.VMEM((n_ex, 2, hi - lo), BF16) for lo, hi in cuts],
            [pltpu.VMEM((n_ex, 2, hi - lo), BF16) for lo, hi in cuts],
            dma((3 + 3 * per_index,)),
            dma((5, n_ex)),
            dma((5, n_ex)),
            dma((n_ex, n_dp)),
            dma((n_ex, n_dp)),
            dma((2, n_dp)),
            dma((2, n_dp)),
        ],
        compiler_params=pltpu.CompilerParams(
            collective_id=0, has_side_effects=True, vmem_limit_bytes=58 * 1024 * 1024
        ),
        cost_estimate=pl.CostEstimate(flops=2 * 10**9, bytes_accessed=29 * 10**6, transcendentals=10**5),
    )(
        prompt_lengths, hidden_in, queries, new_keys, new_values, norm_gain,
        expert_ids, top_logits, key_cache, value_cache, out_weight,
        gate_weight, up_weight, down_weight,
    )


def solution(mesh):
    both = ("expert", "dp")
    placed = (
        P(both, None, None),
        P(both, None, None),
        P(both, None, None),
        P(both, None, None),
        P(both, None, None),
        P(both, None, None),
        P(both),
        P("expert", None),
        P(),
        P("expert", None, None),
        P("expert", None, None),
        P("expert", None, "dp"),
        P("expert", None, "dp"),
        P("expert", "dp", None),
    )
    return jax.shard_map(
        on_device,
        mesh=mesh,
        in_specs=placed,
        out_specs=P(both, None, None),
        check_vma=False,
    )
```

time: 247 us -> 44.8 us (0.18)
  waiting for transfers between devices: 107 us -> 0 us
  Pallas kernels: 0 us -> 42.6 us
  other arithmetic: 32.4 us -> 0 us
  local copies, waits for them, and re-layouts: 29.7 us -> 1.32 us
  matrix products: 26.6 us -> 0 us
  blocking collectives: 24.4 us -> 0 us
  between operations: 14.9 us -> 0.66 us
  starting transfers between devices: 11 us -> 0 us
    unnamed x4 -> x0, waiting for transfers between devices: 94 us -> none
    pallas_call x0 -> x1, Pallas kernels: none -> 42.6 us  [on_device(): pl.pallas_call(functools.partial(layer_kernel, n_dp, n_ex, per_index, cut...]
    dot_general x10 -> x0, matrix products: 26.6 us -> none  [the longest x2 7.8 us: expert_partials(): jnp.dot(row_block, up_weight[local_expert], preferred_element_type=jnp.fl...]
    unnamed x1 -> x0, other arithmetic: 24.4 us -> none
    all_to_all x1 -> x0, blocking collectives: 13.1 us -> none  [on_device(): lax.all_to_all(dispatch, 'expert', split_axis=0, concat_axis=0, tiled=True)]
    all_to_all x2 -> x0, waiting for transfers between devices: 12.9 us -> none  [the longest x1 8.14 us: on_device(): lax.all_to_all(summed.astype(jnp.bfloat16), 'expert', split_axis=0, conca...]
    all_gather x1 -> x0, blocking collectives: 11.3 us -> none  [on_device(): lax.all_gather(arrived, 'dp', axis=0, tiled=True)]
    all_to_all x2 -> x0, starting transfers between devices: 10.9 us -> none  [the longest x1 6.33 us: on_device(): lax.all_to_all(attended, 'expert', split_axis=2, concat_axis=0, tiled=True)]
  transfers between devices with their start and end apart: 4 -> 0, of which waited for: 4 -> 0; matrix products, arithmetic and copies ran while one was open for 1% -> 0% of each run, Pallas kernels for 0% -> 0%
where the time goes in v1:
time: 44.8 us; the launch traced here: 44.5 us
  Pallas kernels  42.6 us (95%)
  local copies, waits for them, and re-layouts  1.32 us (3%)
  between operations  0.66 us (1%)
    pallas_call x1, Pallas kernels, on_device(): pl.pallas_call(functools.partial(layer_kernel, n_dp, n_ex, per_index, cut...  42.6 us
    unnamed x1, local copies, waits for them, and re-layouts  1.32 us

profile of v1, /device:TPU:0, one launch (start us, length us, event | category | flops | bytes accessed | tf_op | source)
XLA Modules:
  0.0 44.5 jit_solution(2753529198576283732)
XLA Ops:
  0.7 42.6 %shard_map.136 = bf16[1,2,2880]{2,1,0:T(2,128)(2,1)} custom-call(s32[1]{0:T(128)S(6)} %copy.16.plen_ref, bf16[1,2,2880]{2,1,0:T(2,128)(2,1)} %hid_ref.1, bf16[1,2,4096]{2,1,0:T(2,128)(2,1)} %q_ref.1, bf16[1,2,512]{2,1,0:T(2,128)(2,1)} %nk_ref.1, bf16[1,2,512]{2,1,0:T(2,128)(2,1)} %nv_ref.1, f32[2880]{0:T(1024)} %gain_ref.1, s32[4,2,4]{2,1,0:T(2,128)} %ids_ref.1, ...), custom_call_target="tpu_custom_call" | custom-call | flops 2000000000 | bytes 29000000 | tf_op jit(solution)/shard_map/pallas_call | solution.py:257
  43.2 1.3 %copy.17 = bf16[1,2,2880]{2,1,0:T(2,128)(2,1)} copy(bf16[1,2,2880]{2,1,0:T(2,128)(2,1)} %shard_map.136) | data formatting | bytes 23040

commit v2 on v1

--- a/solution.py
+++ b/solution.py
@@ -33,11 +33,15 @@
     out_ref,
     kbuf, vbuf, wo, wg, wu, wd,
     qr, att, send_att, recv_att, xa, part, send_proj, recv_proj, resid,
-    xbuf, xs, send_dp, recv_dp, send_out, recv_out,
-    load_sem, ssem, rsem, fssem, frsem, hssem, hrsem,
+    xbuf, xs, xb, tot, send_twin, recv_twin, send_dp, recv_dp, send_out, recv_out,
+    load_sem, ssem, rsem, fssem, frsem, tssem, trsem, hssem, hrsem,
 ):
     me_dp = lax.axis_index("dp")
     me_ex = lax.axis_index("expert")
+    my_z, core = me_ex // 2, lax.rem(me_ex, 2)
+    other, n_z = 1 - core, n_ex // 2
+    per_blk = 16 // (2 * n_z)
+    n_blk = n_dp // per_blk
     steps, width = hid_ref.shape[1], hid_ref.shape[2]
     feats = wo.shape[1]
     pad_at = xbuf.shape[3] - 128
@@ -134,58 +138,70 @@
         send_proj[e] = part[2 * e:2 * e + 2, :].astype(BF16)
     recv_proj[me_ex] = send_proj[me_ex]
     exchange(1, send_proj, recv_proj)
-    xbuf[me_dp, me_ex, :, width:pad_at] = jnp.zeros((steps, pad_at - width), BF16)
-    xbuf[me_dp, me_ex, :, pad_at:] = dense
+    xbuf[me_dp, my_z, :, width:pad_at] = jnp.zeros((steps, pad_at - width), BF16)
+    xbuf[me_dp, my_z, :, pad_at:] = dense
     exchanged(1, send_proj, recv_proj)
     res = hid_ref[0].astype(F32) + jnp.sum(recv_proj[...].astype(F32), axis=0)
     resid[...] = res
     inv = lax.rsqrt(jnp.sum(res * res, axis=1, keepdims=True) / width + 1e-05)
-    xbuf[me_dp, me_ex, :, 0:width] = (res * inv * gain_ref[...].reshape(1, width)).astype(BF16)
-
-    def to_expert(slab, d, peer):
+    xbuf[me_dp, my_z, :, 0:width] = (res * inv * gain_ref[...].reshape(1, width)).astype(BF16)
+
+    def to_z(slab, d, peer):
         return pltpu.make_async_remote_copy(
             xbuf.at[me_dp, slab], xbuf.at[me_dp, slab], ssem.at[2, d], rsem.at[2, slab],
-            device_id=(me_dp, peer), device_id_type=MESH,
+            device_id=(me_dp, 2 * peer + core), device_id_type=MESH,
         )
 
     def to_dp(row, slab, d, peer):
         return pltpu.make_async_remote_copy(
             xbuf.at[row, slab], xbuf.at[row, slab], fssem.at[slab, d], frsem.at[slab, row],
             device_id=(peer, me_ex), device_id_type=MESH,
+        )
+
+    def to_twin(half, b):
+        return pltpu.make_async_remote_copy(
+            xb.at[half * n_blk + b], xb.at[half * n_blk + b], tssem.at[b], trsem.at[b],
+            device_id=(me_dp, 2 * my_z + other), device_id_type=MESH,
         )
 
     def pass_on(slab):
         for d in range(1, n_dp):
             to_dp(me_dp, slab, d, lax.rem(me_dp + d, n_dp)).start()
 
-    for d in range(1, n_ex):
-        to_expert(me_ex, d, lax.rem(me_ex + d, n_ex)).start()
-    pass_on(me_ex)
-    for d in range(1, n_ex):
-        src = lax.rem(me_ex + d, n_ex)
-        to_expert(src, d, src).wait_recv()
+    for d in range(1, n_z):
+        to_z(my_z, d, lax.rem(my_z + d, n_z)).start()
+    pass_on(my_z)
+    for d in range(1, n_z):
+        src = lax.rem(my_z + d, n_z)
+        to_z(src, d, src).wait_recv()
         pass_on(src)
-    for e in range(n_ex):
-        xs[me_dp, 2 * e:2 * e + 2, :] = xbuf[me_dp, e].astype(F32)
+    for d in range(n_dp):
+        row = lax.rem(me_dp + d, n_dp)
+        for z in range(n_z):
+            if d > 0:
+                to_dp(row, z, d, row).wait_recv()
+            xs[d, 2 * z:2 * z + 2, :] = xbuf[row, z].astype(F32)
+        if (d + 1) % per_blk == 0:
+            b = d // per_blk
+            xb[core * n_blk + b] = xs[b * per_blk:(b + 1) * per_blk].reshape(16, pad_at + 128).astype(BF16)
+            to_twin(core, b).start()
+    for d in range(1, n_z):
+        to_z(my_z, d, my_z).wait_send()
     for d in range(1, n_dp):
-        row = lax.rem(me_dp + d, n_dp)
-        for e in range(n_ex):
-            to_dp(row, e, d, row).wait_recv()
-            xs[row, 2 * e:2 * e + 2, :] = xbuf[row, e].astype(F32)
-    for d in range(1, n_ex):
-        to_expert(me_ex, d, me_ex).wait_send()
-    for d in range(1, n_dp):
-        for e in range(n_ex):
-            to_dp(me_dp, e, d, me_dp).wait_send()
-
+        for z in range(n_z):
+            to_dp(me_dp, z, d, me_dp).wait_send()
     for c in loads[3:]:
         c.wait()
-    span = max(1, min(n_dp, 64 // (2 * n_ex)))
-    tokens = span * 2 * n_ex
+    for b in range(n_blk):
+        to_twin(other, b).wait_recv()
+        to_twin(core, b).wait_send()
+
+    span = min(2 * n_blk, 4)
+    tokens = 16 * span
 
     def block(at):
-        x = xs[pl.ds(at, span), :, 0:width].reshape(tokens, width).astype(BF16)
-        shares = xs[pl.ds(at, span), :, pad_at:].reshape(tokens, 128)
+        x = xb[pl.ds(at, span), :, 0:width].reshape(tokens, width)
+        shares = xb[pl.ds(at, span), :, pad_at:].reshape(tokens, 128).astype(F32)
         lane_of = iota((tokens, 128), 1) % 64
         acts, parts = [], []
         for l in range(per_index):
@@ -198,42 +214,63 @@
             total = dot(acts[0], wd[0, :, lo:hi]) * parts[0]
             for l in range(1, per_index):
                 total = total + dot(acts[l], wd[l, :, lo:hi]) * parts[l]
-            send_dp[c][pl.ds(at, span)] = total.reshape(span, 2 * n_ex, hi - lo).astype(BF16)
-            if n_dp == span:
-                scatter(c)
+            tot[c][pl.ds(at, span)] = total.reshape(span, 16, hi - lo)
+            if 2 * n_blk == span:
+                swap(c)
+
+    def twin_sum(c):
+        return pltpu.make_async_remote_copy(
+            send_twin[c], recv_twin[c], tssem.at[n_blk + c], trsem.at[n_blk + c],
+            device_id=(me_dp, 2 * my_z + other), device_id_type=MESH,
+        )
+
+    def swap(c):
+        send_twin[c][...] = tot[c][pl.ds(other * n_blk, n_blk)].astype(BF16)
+        twin_sum(c).start()
 
     def across(c, d, slot):
-        to = lax.rem(me_dp + d, n_dp)
-        return pltpu.make_async_remote_copy(
-            send_dp[c].at[to], recv_dp[c].at[slot], hssem.at[c, d], hrsem.at[c, slot],
-            device_id=(to, me_ex), device_id_type=MESH,
-        )
-
-    def scatter(c):
+        return pltpu.make_async_remote_copy(
+            send_dp[c].at[d], recv_dp[c].at[slot], hssem.at[c, d], hrsem.at[c, slot],
+            device_id=(lax.rem(me_dp + d, n_dp), me_ex), device_id_type=MESH,
+        )
+
+    def along_z(c, d, to, slot):
+        return pltpu.make_async_remote_copy(
+            send_out[c].at[to], recv_out[c].at[slot], ssem.at[3 + c, d], rsem.at[3 + c, slot],
+            device_id=(me_dp, 2 * to + core), device_id_type=MESH,
+        )
+
+    if 2 * n_blk == span:
+        block(0)
+    else:
+        pl.loop(0, 2 * n_blk // span)(lambda i: block(i * span))
+        for c in range(len(cuts)):
+            swap(c)
+    for c, (lo, hi) in enumerate(cuts):
+        twin_sum(c).wait_recv()
+        both = tot[c][pl.ds(core * n_blk, n_blk)] + recv_twin[c][...].astype(F32)
+        send_dp[c][...] = both.reshape(n_dp, 2 * n_z, hi - lo).astype(BF16)
         for d in range(1, n_dp):
             across(c, d, me_dp).start()
-        recv_dp[c][me_dp] = send_dp[c][me_dp]
-
-    if n_dp == span:
-        block(0)
-    else:
-        pl.loop(0, n_dp // span)(lambda i: block(i * span))
-        for c in range(len(cuts)):
-            scatter(c)
-
+        recv_dp[c][me_dp] = send_dp[c][0]
     for c, (lo, hi) in enumerate(cuts):
         for d in range(1, n_dp):
             across(c, d, lax.rem(me_dp + d, n_dp)).wait_recv()
-        part[:, lo:hi] = jnp.sum(recv_dp[c][...].astype(F32), axis=0)
-        for e in range(n_ex):
-            send_out[c][e] = part[2 * e:2 * e + 2, lo:hi].astype(BF16)
-        exchange(3 + c, send_out[c], recv_out[c])
-        recv_out[c][me_ex] = send_out[c][me_ex]
-    for c in range(len(cuts)):
+        part[0:2 * n_z, lo:hi] = jnp.sum(recv_dp[c][...].astype(F32), axis=0)
+        for z in range(n_z):
+            send_out[c][z] = part[2 * z:2 * z + 2, lo:hi].astype(BF16)
+        for d in range(1, n_z):
+            along_z(c, d, lax.rem(my_z + d, n_z), my_z).start()
+        recv_out[c][my_z] = send_out[c][my_z]
+    for c, (lo, hi) in enumerate(cuts):
+        twin_sum(c).wait_send()
         for d in range(1, n_dp):
             across(c, d, me_dp).wait_send()
     for c, (lo, hi) in enumerate(cuts):
-        exchanged(3 + c, send_out[c], recv_out[c])
+        for d in range(1, n_z):
+            src = lax.rem(my_z + d, n_z)
+            along_z(c, d, src, src).wait_recv()
+            along_z(c, d, src, src).wait_send()
         moe = jnp.sum(recv_out[c][...].astype(F32), axis=0)
         out_ref[0, :, lo:hi] = (resid[:, lo:hi] + moe).astype(BF16)
 
@@ -252,6 +289,8 @@
     out_weight = out_weight.T
     padded = -(-width // 128) * 128 + 128
     toks = 2 * n_ex
+    n_z = n_ex // 2
+    n_blk = n_dp * n_ex // 16
     vm, anym = pl.BlockSpec(memory_space=pltpu.VMEM), pl.BlockSpec(memory_space=pl.ANY)
     dma = pltpu.SemaphoreType.DMA
     return pl.pallas_call(
@@ -275,17 +314,23 @@
             pltpu.VMEM((n_ex, 2, width), BF16),
             pltpu.VMEM((n_ex, 2, width), BF16),
             pltpu.VMEM((2, width), F32),
-            pltpu.VMEM((n_dp, n_ex, 2, padded), BF16),
-            pltpu.VMEM((n_dp, toks, padded), F32),
-            [pltpu.VMEM((n_dp, toks, hi - lo), BF16) for lo, hi in cuts],
-            [pltpu.VMEM((n_dp, toks, hi - lo), BF16) for lo, hi in cuts],
-            [pltpu.VMEM((n_ex, 2, hi - lo), BF16) for lo, hi in cuts],
-            [pltpu.VMEM((n_ex, 2, hi - lo), BF16) for lo, hi in cuts],
+            pltpu.VMEM((n_dp, n_z, 2, padded), BF16),
+            pltpu.VMEM((n_dp, n_ex, padded), F32),
+            pltpu.VMEM((2 * n_blk, 16, padded), BF16),
+            [pltpu.VMEM((2 * n_blk, 16, hi - lo), F32) for lo, hi in cuts],
+            [pltpu.VMEM((n_blk, 16, hi - lo), BF16) for lo, hi in cuts],
+            [pltpu.VMEM((n_blk, 16, hi - lo), BF16) for lo, hi in cuts],
+            [pltpu.VMEM((n_dp, n_ex, hi - lo), BF16) for lo, hi in cuts],
+            [pltpu.VMEM((n_dp, n_ex, hi - lo), BF16) for lo, hi in cuts],
+            [pltpu.VMEM((n_z, 2, hi - lo), BF16) for lo, hi in cuts],
+            [pltpu.VMEM((n_z, 2, hi - lo), BF16) for lo, hi in cuts],
             dma((3 + 3 * per_index,)),
             dma((5, n_ex)),
             dma((5, n_ex)),
-            dma((n_ex, n_dp)),
-            dma((n_ex, n_dp)),
+            dma((n_z, n_dp)),
+            dma((n_z, n_dp)),
+            dma((n_blk + 2,)),
+            dma((n_blk + 2,)),
             dma((2, n_dp)),
             dma((2, n_dp)),
         ],

time: 44.8 us -> 42.4 us (0.946)
  Pallas kernels: 42.6 us -> 40.1 us
    pallas_call x1, Pallas kernels: 42.6 us -> 40.1 us  [on_device(): pl.pallas_call(functools.partial(layer_kernel, n_dp, n_ex, per_index, cut...]
where the time goes in v2:
time: 42.4 us; the launch traced here: 42.1 us
  Pallas kernels  40.1 us (95%)
  local copies, waits for them, and re-layouts  1.32 us (3%)
  between operations  0.66 us (2%)
    pallas_call x1, Pallas kernels, on_device(): pl.pallas_call(functools.partial(layer_kernel, n_dp, n_ex, per_index, cut...  40.1 us
    unnamed x1, local copies, waits for them, and re-layouts  1.32 us

profile of v2, /device:TPU:0, one launch (start us, length us, event | category | flops | bytes accessed | tf_op | source)
XLA Modules:
  0.0 42.1 jit_solution(6402326939074628890)
XLA Ops:
  0.7 40.1 %shard_map.136 = bf16[1,2,2880]{2,1,0:T(2,128)(2,1)} custom-call(s32[1]{0:T(128)S(6)} %copy.16.plen_ref, bf16[1,2,2880]{2,1,0:T(2,128)(2,1)} %hid_ref.1, bf16[1,2,4096]{2,1,0:T(2,128)(2,1)} %q_ref.1, bf16[1,2,512]{2,1,0:T(2,128)(2,1)} %nk_ref.1, bf16[1,2,512]{2,1,0:T(2,128)(2,1)} %nv_ref.1, f32[2880]{0:T(1024)} %gain_ref.1, s32[4,2,4]{2,1,0:T(2,128)} %ids_ref.1, ...), custom_call_target="tpu_custom_call" | custom-call | flops 2000000000 | bytes 29000000 | tf_op jit(solution)/shard_map/pallas_call | solution.py:296
  40.8 1.3 %copy.17 = bf16[1,2,2880]{2,1,0:T(2,128)(2,1)} copy(bf16[1,2,2880]{2,1,0:T(2,128)(2,1)} %shard_map.136) | data formatting | bytes 23040
